TPU v7x, 512 devices: a whole 4x8x8 slice. The times are simulated.
512 devices in a mesh: row: 8 (over z), col: 16 (over y, core), layer: 4 (over x).
Axes of the slice: x: 4, y: 8, z: 8, core: 2. Of those that a mesh axis runs over, the one named last changes fastest.
Arguments:
- panel_values: bfloat16 [16384, 8192], P('row', ('layer', 'col')), may hold values from -6 to 6
- slab_values: bfloat16 [8192, 6144], P(('layer', 'row'), 'col'), may hold values from -0.09375 to 0.09375
- pattern_panel: int32 [128, 64], P('row', ('layer', 'col')), may hold values from 0 to 1, as said below
- pattern_result: int32 [128, 48], P(('row', 'layer'), 'col'), may hold values 0 or 1
Outputs:
- product_slab: bfloat16 [16384, 6144], P(('row', 'layer'), 'col')
Inputs may be any that keep to these rules, and one draw needn't show every extreme that they name: `pattern_panel`: in every group of 16 blocks that one device holds of one block column (block rows r * 16 to r * 16 + 15), 1 to 8 are 1; some group reaches this bound: every group of block column 0 has exactly 8.
All inputs are finite; a program needn't handle non-finite values. No bound on the sum of `pattern_result` on one device may be relied on, other than what follows from the above.
Results may differ from a plain program's by a relative error of at most 0.001.
Values may be sent and summed in bfloat16 or wider, within the bound.
A program may use at most 64 MiB of HBM per device.

v0:
```python
import jax
import jax.numpy as jnp
from jax import lax
from jax.sharding import PartitionSpec as P


def per_device(panel_values, slab_values, pattern_panel, pattern_result):
    block = panel_values.shape[1]
    row_blocks = pattern_panel.shape[0]
    gathered = lax.all_gather(slab_values, "row", axis=0, tiled=True)
    flags = pattern_panel[:, 0]
    blocks_here = panel_values.reshape(row_blocks, block, block)
    masked = (blocks_here * flags.astype(jnp.bfloat16)[:, None, None]).reshape(
        row_blocks * block, block
    )
    partial_value = jnp.dot(
        lax.all_gather(masked, "col", axis=1, tiled=True),
        gathered,
        preferred_element_type=jnp.float32,
    )
    shares = lax.psum_scatter(partial_value, "layer", scatter_dimension=0, tiled=True)
    out_blocks = pattern_result.shape[0]
    col_blocks = pattern_result.shape[1]
    keeper = pattern_result.astype(jnp.float32)
    filtered = shares.reshape(out_blocks, block, col_blocks, block) * keeper[:, None, :, None]
    return filtered.reshape(shares.shape).astype(jnp.bfloat16)


def solution(mesh):
    placed = (
        P("row", ("layer", "col")),
        P(("layer", "row"), "col"),
        P("row", ("layer", "col")),
        P(("row", "layer"), "col"),
    )
    return jax.shard_map(
        per_device,
        mesh=mesh,
        in_specs=placed,
        out_specs=P(("row", "layer"), "col"),
        check_vma=False,
    )
```

profile of v0, /device:TPU:1, one launch (start us, length us, event | category | flops | bytes accessed | tf_op | source)
XLA Modules:
  0.0 186.3 jit_solution(16902584694863488766)
XLA Ops:
  6.5 0.0 all-gather.5.cloned.1.call-start
  6.5 0.7 all-gather.5.cloned.1.call-update
  7.3 0.0 all-gather.3.cloned.1.call-start
  7.3 0.7 convert_bitcast_fusion
  8.0 0.1 broadcast_bitcast_fusion
  8.0 2.2 %broadcast_multiply_fusion = bf16[2048,128]{1,0:T(8,128)(2,1)} fusion(bf16[2048,128]{1,0:T(8,128)(2,1)} %param.4, bf16[2048]{0:T(1024)(128)(2,1)S(1)} %broadcast_bitcast_fusion), kind=kLoop, calls=%fused_computation.2 | loop fusion | flops 262144 | bytes 1052672 | tf_op jit(solution)/shard_map/mul | solution.py:13
  10.3 0.0 all-gather.3.cloned.1.call-update
  10.3 0.0 reduce-scatter.2.cloned.1.call-start
  10.3 44.2 %all-gather.5.cloned.1.call-done = bf16[2048,384]{1,0:T(8,128)(2,1)} async-done(((bf16[256,384]{1,0:T(8,128)(2,1)}), bf16[2048,384]{1,0:T(8,128)(2,1)}) %all-gather.5.cloned.1.call-update) | async-done | bytes 1572880 | tf_op jit(solution)/shard_map/all_gather | solution.py:10
  54.5 73.2 %all-gather.3.cloned.1.call-done = bf16[2048,2048]{1,0:T(8,128)(2,1)} async-done(((bf16[2048,128]{1,0:T(8,128)(2,1)}), bf16[2048,2048]{1,0:T(8,128)(2,1)}) %all-gather.3.cloned.1.call-update) | async-done | bytes 8388624 | tf_op jit(solution)/shard_map/all_gather | solution.py:17
  127.7 10.1 %fusion = f32[2048,384]{1,0:T(8,128)} fusion(bf16[2048,2048]{1,0:T(8,128)(2,1)} %all-gather.3.cloned.1.call-done, bf16[2048,384]{1,0:T(8,128)(2,1)} %all-gather.5.cloned.1.call-done), kind=kOutput, calls=%fused_computation.5 | convolution fusion | flops 3221225472 | bytes 13107200 | tf_op jit(solution)/shard_map/dot_general | solution.py:16
  137.8 0.0 copy-start
  137.8 0.0 reduce-scatter.2.cloned.1.call-update
  137.8 0.7 copy-done
  138.4 0.1 copy.5
  138.5 0.2 mul.28
  138.7 0.1 copy.9
  138.8 0.3 copy.6
  139.1 38.8 %reduce-scatter.2.cloned.1.call-done = f32[512,384]{1,0:T(8,128)} async-done(((f32[2048,384]{1,0:T(8,128)}), f32[512,384]{1,0:T(8,128)}) %reduce-scatter.2.cloned.1.call-update) | async-done | bytes 786448 | tf_op jit(solution)/shard_map/reduce_scatter | solution.py:21
  177.8 2.0 %multiply_convert_fusion = bf16[512,384]{1,0:T(8,128)(2,1)} fusion(f32[512,384]{1,0:T(8,128)} %reduce-scatter.2.cloned.1.call-done, f32[512,384]{1,0:T(8,128)S(1)} %copy.6), kind=kLoop, calls=%fused_computation.1 | loop fusion | flops 393216 | bytes 1966080 | tf_op jit(solution)/shard_map/convert_element_type | solution.py:26
  (1 shorter events, 0.0 us)
Async XLA Ops:
  6.5 48.0 %all-gather.5.cloned.1.call-start = ((), (), s32[]{:S(2)}) async-start(), calls=%async_computation.2 | async-start | bytes 1769472 | tf_op jit(solution)/shard_map/all_gather | solution.py:10
  7.3 120.5 %all-gather.3.cloned.1.call-start = ((), (), s32[]{:S(2)}) async-start(), calls=%async_computation.1 | async-start | bytes 8912896 | tf_op jit(solution)/shard_map/all_gather | solution.py:17
  10.3 167.5 %reduce-scatter.2.cloned.1.call-start = ((), (), s32[]{:S(2)}) async-start(), calls=%async_computation.3 | async-start | bytes 3932160 | tf_op jit(solution)/shard_map/reduce_scatter | solution.py:21
  137.8 0.7 copy-start
Sparse Core Ops, SparseCore 0:
  9.4 45.0 all-gather.4
  56.6 71.0 all-gather.2
  137.9 39.8 reduce-scatter.1
where the time goes:
time: 187 us; the launch traced here: 186 us
  waiting for transfers between devices  157 us (84%)
  between operations  13.1 us (7%)
  matrix products  10.1 us (5%)
  other arithmetic  4.83 us (3%)
    all_gather x1, waiting for transfers between devices, per_device(): lax.all_gather(masked, 'col', axis=1, tiled=True)  73.2 us
    all_gather x1, waiting for transfers between devices, per_device(): gathered = lax.all_gather(slab_values, 'row', axis=0, tiled=True)  44.2 us
    reduce_scatter x1, waiting for transfers between devices, per_device(): lax.psum_scatter(partial_value, 'layer', scatter_dimension=0, tiled=True)  38.8 us
    dot_general x1, matrix products, per_device(): jnp.dot(lax.all_gather(masked, 'col', axis=1, tiled=True), gathered, pref...  10.1 us
  transfers between devices with their start and end apart: 3, of which 3 were waited for; matrix products, arithmetic and copies ran while one was open for 2% of the time, Pallas kernels for 0%

commit v1 on v0

--- a/solution.py
+++ b/solution.py
@@ -4,10 +4,20 @@
 from jax.sharding import PartitionSpec as P
 
 
+def gather_by_hops(array, name, dim):
+    n_dev = lax.axis_size(name)
+    block, parts = (array, [array])
+    for _ in range(n_dev - 1):
+        block = lax.ppermute(block, name, [(i, (i + 1) % n_dev) for i in range(n_dev)])
+        parts.insert(0, block)
+    line = jnp.concatenate(parts, axis=dim)
+    return jnp.roll(line, (lax.axis_index(name) + 1) * array.shape[dim], axis=dim)
+
+
 def per_device(panel_values, slab_values, pattern_panel, pattern_result):
     block = panel_values.shape[1]
     row_blocks = pattern_panel.shape[0]
-    gathered = lax.all_gather(slab_values, "row", axis=0, tiled=True)
+    gathered = gather_by_hops(slab_values, "row", 0)
     flags = pattern_panel[:, 0]
     blocks_here = panel_values.reshape(row_blocks, block, block)
     masked = (blocks_here * flags.astype(jnp.bfloat16)[:, None, None]).reshape(

time: 187 us -> 152 us (0.81)
  waiting for transfers between devices: 157 us -> 94.3 us
  starting transfers between devices: 0.08 us -> 16.3 us
  local copies, waits for them, and re-layouts: 1.31 us -> 12.5 us
    all_gather x1, waiting for transfers between devices: 73.2 us -> 0.01 us  [per_device(): lax.all_gather(masked, 'col', axis=1, tiled=True)]
    ppermute x0 -> x7, waiting for transfers between devices: none -> 48.1 us  [gather_by_hops(): lax.ppermute(block, name, [(i, (i + 1) % n_dev) for i in range(n_dev)])]
    all_gather x1 -> x0, waiting for transfers between devices: 44.2 us -> none  [per_device(): gathered = lax.all_gather(slab_values, 'row', axis=0, tiled=True)]
    ppermute x0 -> x7, starting transfers between devices: none -> 16.3 us  [gather_by_hops(): lax.ppermute(block, name, [(i, (i + 1) % n_dev) for i in range(n_dev)])]
    unnamed x3 -> x20, local copies, waits for them, and re-layouts: 0.71 us -> 11.2 us
    reduce_scatter x1, waiting for transfers between devices: 38.8 us -> 46.2 us  [per_device(): lax.psum_scatter(partial_value, 'layer', scatter_dimension=0, tiled=True)]
  transfers between devices with their start and end apart: 3 -> 9, of which waited for: 3 -> 8; matrix products, arithmetic and copies ran while one was open for 2% -> 8% of each run, Pallas kernels for 0% -> 0%
where the time goes in v1:
time: 152 us
  waiting for transfers between devices  94.3 us (62%)
  starting transfers between devices  16.3 us (11%)
  between operations  13.5 us (9%)
  local copies, waits for them, and re-layouts  12.5 us (8%)
  matrix products  10 us (7%)
  other arithmetic  4.85 us (3%)
    ppermute x7, waiting for transfers between devices, gather_by_hops(): lax.ppermute(block, name, [(i, (i + 1) % n_dev) for i in range(n_dev)])  48.1 us
    reduce_scatter x1, waiting for transfers between devices, per_device(): lax.psum_scatter(partial_value, 'layer', scatter_dimension=0, tiled=True)  46.2 us
    ppermute x7, starting transfers between devices, gather_by_hops(): lax.ppermute(block, name, [(i, (i + 1) % n_dev) for i in range(n_dev)])  16.3 us
    unnamed x20, local copies, waits for them, and re-layouts  11.2 us
    dot_general x1, matrix products, per_device(): jnp.dot(lax.all_gather(masked, 'col', axis=1, tiled=True), gathered, pref...  10 us
  transfers between devices with their start and end apart: 9, of which 8 were waited for; matrix products, arithmetic and copies ran while one was open for 8% of the time, Pallas kernels for 0%

profile of v1, /device:TPU:1, one launch (start us, length us, event | category | flops | bytes accessed | tf_op | source)
XLA Modules:
  0.0 151.6 jit_solution(17632208486148907574)
XLA Ops:
  6.5 0.0 copy-start
  6.5 0.0 all-gather.2.cloned.1.call-start
  6.5 0.7 convert_bitcast_fusion
  7.2 0.1 broadcast_bitcast_fusion
  7.3 2.2 %broadcast_multiply_fusion = bf16[2048,128]{1,0:T(8,128)(2,1)} fusion(bf16[2048,128]{1,0:T(8,128)(2,1)} %param.4, bf16[2048]{0:T(1024)(128)(2,1)S(1)} %broadcast_bitcast_fusion), kind=kLoop, calls=%fused_computation.4 | loop fusion | flops 262144 | bytes 1052672 | tf_op jit(solution)/shard_map/mul | solution.py:23
  9.5 0.0 all-gather.2.cloned.1.call-update
  9.5 0.0 reduce-scatter.2.cloned.1.call-start
  9.6 4.8 %collective-permute-start = (bf16[256,384]{1,0:T(8,128)(2,1)}, bf16[256,384]{1,0:T(8,128)(2,1)S(1)}, u32[]{:S(2)}, u32[]{:S(2)}) collective-permute-start(bf16[256,384]{1,0:T(8,128)(2,1)} %param.5), channel_id=1, source_target_pairs={{0,64},{64,128},{128,192},{192,256},{256,320},{320,384},{384,448},... | collective-permute-start | bytes 589832 | tf_op jit(solution)/shard_map/ppermute | solution.py:11
  14.4 11.5 %collective-permute-done = bf16[256,384]{1,0:T(8,128)(2,1)S(1)} collective-permute-done((bf16[256,384]{1,0:T(8,128)(2,1)}, bf16[256,384]{1,0:T(8,128)(2,1)S(1)}, u32[]{:S(2)}, u32[]{:S(2)}) %collective-permute-start) | collective-permute-done | bytes 196640 | tf_op jit(solution)/shard_map/ppermute | solution.py:11
  25.9 1.9 %collective-permute-start.1 = (bf16[256,384]{1,0:T(8,128)(2,1)S(1)}, bf16[256,384]{1,0:T(8,128)(2,1)S(1)}, u32[]{:S(2)}, u32[]{:S(2)}) collective-permute-start(bf16[256,384]{1,0:T(8,128)(2,1)S(1)} %collective-permute-done), channel_id=1, source_target_pairs={{0,64},{64,128},{128,192},{192,256},{256,320},{320,384},{384,448},... | collective-permute-start | bytes 589832 | tf_op jit(solution)/shard_map/ppermute | solution.py:11
  27.8 6.4 %collective-permute-done.1 = bf16[256,384]{1,0:T(8,128)(2,1)S(1)} collective-permute-done((bf16[256,384]{1,0:T(8,128)(2,1)S(1)}, bf16[256,384]{1,0:T(8,128)(2,1)S(1)}, u32[]{:S(2)}, u32[]{:S(2)}) %collective-permute-start.1) | collective-permute-done | bytes 196640 | tf_op jit(solution)/shard_map/ppermute | solution.py:11
  34.3 1.9 %collective-permute-start.2 = (bf16[256,384]{1,0:T(8,128)(2,1)S(1)}, bf16[256,384]{1,0:T(8,128)(2,1)S(1)}, u32[]{:S(2)}, u32[]{:S(2)}) collective-permute-start(bf16[256,384]{1,0:T(8,128)(2,1)S(1)} %collective-permute-done.1), channel_id=1, source_target_pairs={{0,64},{64,128},{128,192},{192,256},{256,320},{320,384},{384,448},... | collective-permute-start | bytes 589832 | tf_op jit(solution)/shard_map/ppermute | solution.py:11
  36.2 6.1 %collective-permute-done.2 = bf16[256,384]{1,0:T(8,128)(2,1)S(1)} collective-permute-done((bf16[256,384]{1,0:T(8,128)(2,1)S(1)}, bf16[256,384]{1,0:T(8,128)(2,1)S(1)}, u32[]{:S(2)}, u32[]{:S(2)}) %collective-permute-start.2) | collective-permute-done | bytes 196640 | tf_op jit(solution)/shard_map/ppermute | solution.py:11
  42.3 1.9 %collective-permute-start.3 = (bf16[256,384]{1,0:T(8,128)(2,1)S(1)}, bf16[256,384]{1,0:T(8,128)(2,1)S(1)}, u32[]{:S(2)}, u32[]{:S(2)}) collective-permute-start(bf16[256,384]{1,0:T(8,128)(2,1)S(1)} %collective-permute-done.2), channel_id=1, source_target_pairs={{0,64},{64,128},{128,192},{192,256},{256,320},{320,384},{384,448},... | collective-permute-start | bytes 589832 | tf_op jit(solution)/shard_map/ppermute | solution.py:11
  44.2 6.1 %collective-permute-done.3 = bf16[256,384]{1,0:T(8,128)(2,1)S(1)} collective-permute-done((bf16[256,384]{1,0:T(8,128)(2,1)S(1)}, bf16[256,384]{1,0:T(8,128)(2,1)S(1)}, u32[]{:S(2)}, u32[]{:S(2)}) %collective-permute-start.3) | collective-permute-done | bytes 196640 | tf_op jit(solution)/shard_map/ppermute | solution.py:11
  50.3 1.9 %collective-permute-start.4 = (bf16[256,384]{1,0:T(8,128)(2,1)S(1)}, bf16[256,384]{1,0:T(8,128)(2,1)S(1)}, u32[]{:S(2)}, u32[]{:S(2)}) collective-permute-start(bf16[256,384]{1,0:T(8,128)(2,1)S(1)} %collective-permute-done.3), channel_id=1, source_target_pairs={{0,64},{64,128},{128,192},{192,256},{256,320},{320,384},{384,448},... | collective-permute-start | bytes 589832 | tf_op jit(solution)/shard_map/ppermute | solution.py:11
  52.2 6.1 %collective-permute-done.4 = bf16[256,384]{1,0:T(8,128)(2,1)S(1)} collective-permute-done((bf16[256,384]{1,0:T(8,128)(2,1)S(1)}, bf16[256,384]{1,0:T(8,128)(2,1)S(1)}, u32[]{:S(2)}, u32[]{:S(2)}) %collective-permute-start.4) | collective-permute-done | bytes 196640 | tf_op jit(solution)/shard_map/ppermute | solution.py:11
  58.3 1.9 %collective-permute-start.5 = (bf16[256,384]{1,0:T(8,128)(2,1)S(1)}, bf16[256,384]{1,0:T(8,128)(2,1)S(1)}, u32[]{:S(2)}, u32[]{:S(2)}) collective-permute-start(bf16[256,384]{1,0:T(8,128)(2,1)S(1)} %collective-permute-done.4), channel_id=1, source_target_pairs={{0,64},{64,128},{128,192},{192,256},{256,320},{320,384},{384,448},... | collective-permute-start | bytes 589832 | tf_op jit(solution)/shard_map/ppermute | solution.py:11
  60.2 6.1 %collective-permute-done.5 = bf16[256,384]{1,0:T(8,128)(2,1)S(1)} collective-permute-done((bf16[256,384]{1,0:T(8,128)(2,1)S(1)}, bf16[256,384]{1,0:T(8,128)(2,1)S(1)}, u32[]{:S(2)}, u32[]{:S(2)}) %collective-permute-start.5) | collective-permute-done | bytes 196640 | tf_op jit(solution)/shard_map/ppermute | solution.py:11
  66.3 1.9 %collective-permute-start.6 = (bf16[256,384]{1,0:T(8,128)(2,1)S(1)}, bf16[256,384]{1,0:T(8,128)(2,1)S(1)}, u32[]{:S(2)}, u32[]{:S(2)}) collective-permute-start(bf16[256,384]{1,0:T(8,128)(2,1)S(1)} %collective-permute-done.5), channel_id=1, source_target_pairs={{0,64},{64,128},{128,192},{192,256},{256,320},{320,384},{384,448},... | collective-permute-start | bytes 589832 | tf_op jit(solution)/shard_map/ppermute | solution.py:11
  68.3 5.8 %collective-permute-done.6 = bf16[256,384]{1,0:T(8,128)(2,1)S(1)} collective-permute-done((bf16[256,384]{1,0:T(8,128)(2,1)S(1)}, bf16[256,384]{1,0:T(8,128)(2,1)S(1)}, u32[]{:S(2)}, u32[]{:S(2)}) %collective-permute-start.6) | collective-permute-done | bytes 196640 | tf_op jit(solution)/shard_map/ppermute | solution.py:11
  74.1 0.7 constant_dynamic-update-slice_fusion.15
  74.8 0.7 constant_dynamic-update-slice_fusion.14
  75.5 0.7 constant_dynamic-update-slice_fusion.13
  76.1 0.7 constant_dynamic-update-slice_fusion.12
  76.9 0.7 constant_dynamic-update-slice_fusion.11
  77.6 0.7 constant_dynamic-update-slice_fusion.10
  78.3 0.7 constant_dynamic-update-slice_fusion.9
  79.0 0.0 copy-done
  79.0 0.7 constant_dynamic-update-slice_fusion.8
  79.7 0.7 constant_dynamic-update-slice_fusion.7
  80.4 0.7 constant_dynamic-update-slice_fusion.6
  81.1 0.7 constant_dynamic-update-slice_fusion.5
  81.8 0.7 constant_dynamic-update-slice_fusion.4
  82.5 0.7 constant_dynamic-update-slice_fusion.3
  83.2 0.7 constant_dynamic-update-slice_fusion.2
  83.9 0.7 constant_dynamic-update-slice_fusion.1
  84.6 0.7 constant_dynamic-update-slice_fusion
  85.3 0.0 all-gather.2.cloned.1.call-done
  85.3 10.0 %fusion = f32[2048,384]{1,0:T(8,128)} fusion(bf16[2048,2048]{1,0:T(8,128)(2,1)} %all-gather.2.cloned.1.call-done, bf16[4096,384]{1,0:T(8,128)(2,1)} %constant_dynamic-update-slice_fusion, s32[]{:T(128)S(6)} %select_n.14), kind=kOutput, calls=%fused_computation | convolution fusion | flops 3221225472 | bytes 13107204 | tf_op jit(solution)/shard_map/dot_general | solution.py:26
  95.3 0.0 reduce-scatter.2.cloned.1.call-update
  95.3 0.7 copy-done.1
  96.0 0.1 copy.5
  96.1 0.2 mul.32
  96.3 0.1 copy.9
  96.3 0.3 copy.6
  96.6 46.2 %reduce-scatter.2.cloned.1.call-done = f32[512,384]{1,0:T(8,128)} async-done(((f32[2048,384]{1,0:T(8,128)}), f32[512,384]{1,0:T(8,128)}) %reduce-scatter.2.cloned.1.call-update) | async-done | bytes 786448 | tf_op jit(solution)/shard_map/reduce_scatter | solution.py:31
  142.8 2.0 %multiply_convert_fusion = bf16[512,384]{1,0:T(8,128)(2,1)} fusion(f32[512,384]{1,0:T(8,128)} %reduce-scatter.2.cloned.1.call-done, f32[512,384]{1,0:T(8,128)S(1)} %copy.6), kind=kLoop, calls=%fused_computation.3 | loop fusion | flops 393216 | bytes 1966080 | tf_op jit(solution)/shard_map/convert_element_type | solution.py:36
  (2 shorter events, 0.0 us)
Async XLA Ops:
  6.5 72.4 %copy-start = (bf16[256,384]{1,0:T(8,128)(2,1)S(1)}, bf16[256,384]{1,0:T(8,128)(2,1)}, u32[]{:S(2)}) copy-start(bf16[256,384]{1,0:T(8,128)(2,1)} %param.5) | copy-start | bytes 589828
  6.5 78.8 %all-gather.2.cloned.1.call-start = ((), (), s32[]{:S(2)}) async-start(), calls=%async_computation.1 | async-start | bytes 8912896 | tf_op jit(solution)/shard_map/all_gather | solution.py:27
  9.5 133.3 %reduce-scatter.2.cloned.1.call-start = ((), (), s32[]{:S(2)}) async-start(), calls=%async_computation.2 | async-start | bytes 3932160 | tf_op jit(solution)/shard_map/reduce_scatter | solution.py:31
  9.6 16.3 %collective-permute-start = (bf16[256,384]{1,0:T(8,128)(2,1)}, bf16[256,384]{1,0:T(8,128)(2,1)S(1)}, u32[]{:S(2)}, u32[]{:S(2)}) collective-permute-start(bf16[256,384]{1,0:T(8,128)(2,1)} %param.5), channel_id=1, source_target_pairs={{0,64},{64,128},{128,192},{192,256},{256,320},{320,384},{384,448},... | collective-permute-start | bytes 589832 | tf_op jit(solution)/shard_map/ppermute | solution.py:11
  25.9 8.4 %collective-permute-start.1 = (bf16[256,384]{1,0:T(8,128)(2,1)S(1)}, bf16[256,384]{1,0:T(8,128)(2,1)S(1)}, u32[]{:S(2)}, u32[]{:S(2)}) collective-permute-start(bf16[256,384]{1,0:T(8,128)(2,1)S(1)} %collective-permute-done), channel_id=1, source_target_pairs={{0,64},{64,128},{128,192},{192,256},{256,320},{320,384},{384,448},... | collective-permute-start | bytes 589832 | tf_op jit(solution)/shard_map/ppermute | solution.py:11
  34.3 8.0 %collective-permute-start.2 = (bf16[256,384]{1,0:T(8,128)(2,1)S(1)}, bf16[256,384]{1,0:T(8,128)(2,1)S(1)}, u32[]{:S(2)}, u32[]{:S(2)}) collective-permute-start(bf16[256,384]{1,0:T(8,128)(2,1)S(1)} %collective-permute-done.1), channel_id=1, source_target_pairs={{0,64},{64,128},{128,192},{192,256},{256,320},{320,384},{384,448},... | collective-permute-start | bytes 589832 | tf_op jit(solution)/shard_map/ppermute | solution.py:11
  42.3 8.0 %collective-permute-start.3 = (bf16[256,384]{1,0:T(8,128)(2,1)S(1)}, bf16[256,384]{1,0:T(8,128)(2,1)S(1)}, u32[]{:S(2)}, u32[]{:S(2)}) collective-permute-start(bf16[256,384]{1,0:T(8,128)(2,1)S(1)} %collective-permute-done.2), channel_id=1, source_target_pairs={{0,64},{64,128},{128,192},{192,256},{256,320},{320,384},{384,448},... | collective-permute-start | bytes 589832 | tf_op jit(solution)/shard_map/ppermute | solution.py:11
  50.3 8.0 %collective-permute-start.4 = (bf16[256,384]{1,0:T(8,128)(2,1)S(1)}, bf16[256,384]{1,0:T(8,128)(2,1)S(1)}, u32[]{:S(2)}, u32[]{:S(2)}) collective-permute-start(bf16[256,384]{1,0:T(8,128)(2,1)S(1)} %collective-permute-done.3), channel_id=1, source_target_pairs={{0,64},{64,128},{128,192},{192,256},{256,320},{320,384},{384,448},... | collective-permute-start | bytes 589832 | tf_op jit(solution)/shard_map/ppermute | solution.py:11
  58.3 8.0 %collective-permute-start.5 = (bf16[256,384]{1,0:T(8,128)(2,1)S(1)}, bf16[256,384]{1,0:T(8,128)(2,1)S(1)}, u32[]{:S(2)}, u32[]{:S(2)}) collective-permute-start(bf16[256,384]{1,0:T(8,128)(2,1)S(1)} %collective-permute-done.4), channel_id=1, source_target_pairs={{0,64},{64,128},{128,192},{192,256},{256,320},{320,384},{384,448},... | collective-permute-start | bytes 589832 | tf_op jit(solution)/shard_map/ppermute | solution.py:11
  66.3 7.7 %collective-permute-start.6 = (bf16[256,384]{1,0:T(8,128)(2,1)S(1)}, bf16[256,384]{1,0:T(8,128)(2,1)S(1)}, u32[]{:S(2)}, u32[]{:S(2)}) collective-permute-start(bf16[256,384]{1,0:T(8,128)(2,1)S(1)} %collective-permute-done.5), channel_id=1, source_target_pairs={{0,64},{64,128},{128,192},{192,256},{256,320},{320,384},{384,448},... | collective-permute-start | bytes 589832 | tf_op jit(solution)/shard_map/ppermute | solution.py:11
  95.3 0.7 copy-start.1
Sparse Core Ops, SparseCore 0:
  9.7 73.9 all-gather.1
  95.5 47.2 reduce-scatter.1
